TPU v7x, 256 devices: a whole 4x4x8 slice. The times are simulated.
256 devices in a mesh: dp: 16 (over x_lo, y, core), tensor: 16 (over z, x_hi).
Axes of the slice: x: 4 (x_hi: 2, x_lo: 2; x = x_hi * 2 + x_lo), y: 4, z: 8, core: 2. Of those that a mesh axis runs over, the one named last changes fastest.
Arguments:
- tokens: bfloat16 [8192, 4096], P(('dp', 'tensor')), may hold values from -24 to 24
- cotangent: bfloat16 [8192, 4096], P(('dp', 'tensor')), may hold values from -24 to 24
- w_in: bfloat16 [4096, 8192], P(None, 'tensor'), may hold values from -0.09375 to 0.09375
- w_out: bfloat16 [8192, 4096], P('tensor'), may hold values from -0.0625 to 0.0625
Outputs:
- grad_tokens: bfloat16 [8192, 4096], P(('dp', 'tensor'))
- grad_in: bfloat16 [4096, 8192], P('dp', 'tensor')
- grad_out: bfloat16 [8192, 4096], P('tensor', 'dp')
All inputs are finite; a program needn't handle non-finite values.
Results may differ from a plain program's by a relative error of at most 0.023.
Values may be sent and summed in bfloat16 or wider, within the bound.
A program may use at most 128 MiB of HBM per device.

v0:
```python
import math

import jax
import jax.numpy as jnp
from jax import lax
from jax.sharding import PartitionSpec as P

cubic_coef = 0.044715
root_coef = 0.7978845608028654


def gelu_parts(pre):
    inner = root_coef * (pre + cubic_coef * pre * pre * pre)
    tangent = jnp.tanh(inner)
    value = 0.5 * pre * (1.0 + tangent)
    slope = 0.5 * (1.0 + tangent) + 0.5 * pre * (1.0 - tangent * tangent) * root_coef * (
        1.0 + 3.0 * cubic_coef * pre * pre
    )
    return (value, slope)


def forward_rows(piece_x, piece_dy, w_in, w_out):
    pre = jnp.dot(piece_x, w_in, preferred_element_type=jnp.float32)
    value, slope = gelu_parts(pre)
    act = value.astype(jnp.bfloat16)
    dact = lax.dot_general(
        piece_dy, w_out, (((1,), (1,)), ((), ())), preferred_element_type=jnp.float32
    )
    dpre = (dact * slope).astype(jnp.bfloat16)
    return (act, dpre)


def weight_grads(group_x, group_dy, act, dpre):
    part_in = lax.dot_general(
        group_x, dpre, (((0,), (0,)), ((), ())), preferred_element_type=jnp.float32
    )
    part_out = lax.dot_general(
        act, group_dy, (((0,), (0,)), ((), ())), preferred_element_type=jnp.float32
    )
    return (part_in, part_out)


def local(tokens, cotangent, w_in, w_out):
    shard_rows = tokens.shape[0]
    tensor_count = lax.axis_size("tensor")
    data_count = lax.axis_size("dp")
    group_rows = shard_rows * tensor_count
    scale_factor = 1.0 / math.sqrt(group_rows * data_count)
    gathered_x, gathered_dy = (
        lax.all_gather(tokens, "tensor", axis=0, tiled=True),
        lax.all_gather(cotangent, "tensor", axis=0, tiled=True),
    )
    act, dpre = forward_rows(gathered_x, gathered_dy, w_in, w_out)
    sum_in, sum_out = weight_grads(gathered_x, gathered_dy, act, dpre)
    grad_tokens = lax.psum_scatter(
        lax.dot_general(
            dpre, w_in, (((1,), (1,)), ((), ())), preferred_element_type=jnp.float32
        ).astype(jnp.bfloat16),
        "tensor",
        scatter_dimension=0,
        tiled=True,
    )
    scaled_in = sum_in * scale_factor
    scaled_out = sum_out * scale_factor
    grad_in, grad_out = (
        lax.psum_scatter(
            scaled_in.astype(jnp.bfloat16), "dp", scatter_dimension=0, tiled=True
        ).astype(jnp.float32),
        lax.psum_scatter(
            scaled_out.astype(jnp.bfloat16), "dp", scatter_dimension=1, tiled=True
        ).astype(jnp.float32),
    )
    return (grad_tokens, grad_in.astype(jnp.bfloat16), grad_out.astype(jnp.bfloat16))


def solution(mesh):
    placed = (
        P(("dp", "tensor"), None),
        P(("dp", "tensor"), None),
        P(None, "tensor"),
        P("tensor", None),
    )
    return jax.shard_map(
        local,
        mesh=mesh,
        in_specs=placed,
        out_specs=(P(("dp", "tensor"), None), P("dp", "tensor"), P("tensor", "dp")),
        check_vma=False,
    )
```

profile of v0, /device:TPU:1, one launch (start us, length us, event | category | flops | bytes accessed | tf_op | source)
XLA Modules:
  0.0 578.8 jit_solution(1194466173585349230)
XLA Ops:
  7.2 0.0 all-gather.5.cloned.1.call-start
  7.2 0.7 all-gather.5.cloned.1.call-update
  7.9 0.0 all-gather.3.cloned.1.call-start
  7.9 0.7 all-gather.3.cloned.1.call-update
  8.6 0.0 reduce-scatter.6.cloned.1.call-start
  8.7 102.5 %all-gather.5.cloned.1.call-done = bf16[512,4096]{1,0:T(8,128)(2,1)} async-done(((bf16[32,4096]{1,0:T(8,128)(2,1)}), bf16[512,4096]{1,0:T(8,128)(2,1)}) %all-gather.5.cloned.1.call-update) | async-done | bytes 4194320 | tf_op jit(solution)/shard_map/all_gather | solution.py:50
  111.2 5.8 fusion.15
  117.0 93.4 %all-gather.3.cloned.1.call-done = bf16[512,4096]{1,0:T(8,128)(2,1)} async-done(((bf16[32,4096]{1,0:T(8,128)(2,1)}), bf16[512,4096]{1,0:T(8,128)(2,1)}) %all-gather.3.cloned.1.call-update) | async-done | bytes 4194320 | tf_op jit(solution)/shard_map/all_gather | solution.py:51
  210.3 0.0 copy-start
  210.3 6.4 %fusion.1 = bf16[512,512]{1,0:T(8,128)(2,1)S(1)} fusion(bf16[512,4096]{1,0:T(8,128)(2,1)} %all-gather.3.cloned.1.call-done, bf16[512,4096]{1,0:T(8,128)(2,1)} %param.7, f32[512,512]{1,0:T(8,128)S(1)} %fusion.15), kind=kOutput, calls=%fused_computation.7 | convolution fusion | flops 2152464384 | bytes 9961472 | tf_op jit(solution)/shard_map/dot_general | solution.py:26
  216.8 0.0 copy-done
  216.8 4.4 fusion
  221.2 0.0 reduce-scatter.6.cloned.1.call-update
  221.2 0.0 reduce-scatter.8.cloned.1.call-start
  221.3 6.6 %multiply_convert_fusion = bf16[512,4096]{1,0:T(8,128)(2,1)} fusion(bf16[512,4096]{1,0:T(8,128)(2,1)} %all-gather.3.cloned.1.call-done, f32[512,512]{1,0:T(8,128)S(1)} %fusion.15), kind=kOutput, calls=%fused_computation | convolution fusion | flops 2154037248 | bytes 9437184 | tf_op jit(solution)/shard_map/dot_general | solution.py:37
  227.9 0.0 reduce-scatter.8.cloned.1.call-update
  227.9 0.0 reduce-scatter.4.cloned.1.call-start
  228.0 6.5 %convolution_convert_fusion = bf16[512,4096]{1,0:T(8,128)(2,1)} fusion(bf16[512,512]{1,0:T(8,128)(2,1)S(1)} %fusion.1, bf16[4096,512]{1,0:T(8,128)(2,1)} %param.6), kind=kOutput, calls=%fused_computation.2 | convolution fusion | flops 2149580800 | bytes 8912896 | tf_op jit(solution)/shard_map/dot_general | solution.py:56
  234.5 0.0 reduce-scatter.4.cloned.1.call-update
  234.5 52.6 %reduce-scatter.6.cloned.1.call-done = bf16[256,512]{0,1:T(8,128)(2,1)} async-done(((bf16[4096,512]{0,1:T(8,128)(2,1)}), bf16[256,512]{0,1:T(8,128)(2,1)}) %reduce-scatter.6.cloned.1.call-update) | async-done | bytes 262160 | tf_op jit(solution)/shard_map/reduce_scatter | solution.py:66
  287.1 1.8 copy.7
  288.9 69.2 %reduce-scatter.8.cloned.1.call-done = bf16[512,256]{1,0:T(8,128)(2,1)} async-done(((bf16[512,4096]{1,0:T(8,128)(2,1)}), bf16[512,256]{1,0:T(8,128)(2,1)}) %reduce-scatter.8.cloned.1.call-update) | async-done | bytes 262160 | tf_op jit(solution)/shard_map/reduce_scatter | solution.py:69
  358.0 214.2 %reduce-scatter.4.cloned.1.call-done = bf16[32,4096]{1,0:T(8,128)(2,1)} async-done(((bf16[512,4096]{1,0:T(8,128)(2,1)}), bf16[32,4096]{1,0:T(8,128)(2,1)}) %reduce-scatter.4.cloned.1.call-update) | async-done | bytes 262160 | tf_op jit(solution)/shard_map/reduce_scatter | solution.py:55
Async XLA Ops:
  7.2 104.0 %all-gather.5.cloned.1.call-start = ((), (), s32[]{:S(2)}) async-start(), calls=%async_computation.4 | async-start | bytes 4456448 | tf_op jit(solution)/shard_map/all_gather | solution.py:50
  7.9 202.5 %all-gather.3.cloned.1.call-start = ((), (), s32[]{:S(2)}) async-start(), calls=%async_computation.3 | async-start | bytes 4456448 | tf_op jit(solution)/shard_map/all_gather | solution.py:51
  8.6 278.4 %reduce-scatter.6.cloned.1.call-start = ((), (), s32[]{:S(2)}) async-start(), calls=%async_computation.6 | async-start | bytes 4456448 | tf_op jit(solution)/shard_map/reduce_scatter | solution.py:66
  210.3 6.4 %copy-start = (bf16[512,4096]{1,0:T(8,128)(2,1)S(1)}, bf16[512,4096]{1,0:T(8,128)(2,1)}, u32[]{:S(2)}) copy-start(bf16[512,4096]{1,0:T(8,128)(2,1)} %all-gather.5.cloned.1.call-done) | copy-start | bytes 12582916
  221.2 136.8 %reduce-scatter.8.cloned.1.call-start = ((), (), s32[]{:S(2)}) async-start(), calls=%async_computation.7 | async-start | bytes 4456448 | tf_op jit(solution)/shard_map/reduce_scatter | solution.py:69
  227.9 344.3 %reduce-scatter.4.cloned.1.call-start = ((), (), s32[]{:S(2)}) async-start(), calls=%async_computation.5 | async-start | bytes 4456448 | tf_op jit(solution)/shard_map/reduce_scatter | solution.py:55
Sparse Core Ops, SparseCore 0:
  10.6 100.5 all-gather.4
  113.8 96.5 all-gather.2
  221.4 65.6 reduce-scatter.5
  290.0 67.9 reduce-scatter.7
  362.5 209.7 reduce-scatter.3
where the time goes:
time: 583 us; the launch traced here: 579 us
  waiting for transfers between devices  533 us (91%)
  matrix products  29.8 us (5%)
  between operations  13.8 us (2%)
    reduce_scatter x1, waiting for transfers between devices, local(): lax.psum_scatter(lax.dot_general(dpre, w_in, (((1,), (1,)), ((), ())), pr...  214 us
    all_gather x1, waiting for transfers between devices, local(): lax.all_gather(tokens, 'tensor', axis=0, tiled=True)  102 us
    all_gather x1, waiting for transfers between devices, local(): lax.all_gather(cotangent, 'tensor', axis=0, tiled=True)  93.4 us
    reduce_scatter x1, waiting for transfers between devices, local(): lax.psum_scatter(scaled_out.astype(jnp.bfloat16), 'dp', scatter_dimension...  69.2 us
    reduce_scatter x1, waiting for transfers between devices, local(): lax.psum_scatter(scaled_in.astype(jnp.bfloat16), 'dp', scatter_dimension=...  52.6 us
  transfers between devices with their start and end apart: 5, of which 5 were waited for; matrix products, arithmetic and copies ran while one was open for 4% of the time, Pallas kernels for 0%

commit v1 on v0

v1 whole, which is shorter than its diff:
```python
import functools
import math

import jax
import jax.numpy as jnp
from jax import lax
from jax.experimental import pallas as pl
from jax.experimental.pallas import tpu as pltpu
from jax.sharding import PartitionSpec as P

MESH = pl.DeviceIdType.MESH
F32, BF16 = jnp.float32, jnp.bfloat16
CUBIC, ROOT = 0.044715, 0.7978845608028654

SHARD = 32
HALF = SHARD // 2
CHUNK = 4 * SHARD
Z, Y = 8, 4
OWN, PAIR = 0, 1
BELOW, ABOVE = 0, 1


def gelu_parts(pre):
    tangent = jnp.tanh(ROOT * (pre + CUBIC * pre * pre * pre))
    value = 0.5 * pre * (1.0 + tangent)
    slope = 0.5 * (1.0 + tangent) + 0.5 * pre * (1.0 - tangent * tangent) * ROOT * (
        1.0 + 3.0 * CUBIC * pre * pre
    )
    return value, slope


def row_of(side, way, hop):
    if hop == 0:
        return 3 * CHUNK + side * SHARD
    if hop == 4:
        return 3 * CHUNK + (2 + side) * SHARD
    return (hop - 1) * CHUNK + (2 * way + side) * SHARD


def nt(a, b):
    return lax.dot_general(a, b, (((1,), (1,)), ((), ())), preferred_element_type=F32)


class Links:
    def __init__(self, send_sems, recv_sems):
        self.send_sems, self.recv_sems = send_sems, recv_sems
        self.copies = {}

    def send(self, key, src, dst, device):
        at = len(self.copies)
        copy = pltpu.make_async_remote_copy(
            src_ref=src,
            dst_ref=dst,
            send_sem=self.send_sems.at[at],
            recv_sem=self.recv_sems.at[at],
            device_id=device,
            device_id_type=MESH,
        )
        copy.start()
        self.copies[key] = copy

    def arrived(self, key):
        self.copies[key].wait_recv()

    def finish(self):
        for copy in self.copies.values():
            copy.wait_send()


MESSAGES = 120


def kernel(
    tokens_ref, cotangent_ref, w_in_ref, w_out_ref,
    gtok_ref, gin_ref, gout_ref,
    tok, cot, win, wout, dpre, actt, dpret, gx,
    from_z, from_pair, from_pair_end,
    core_out, core_in, part_in, part_out, xl_in, xl_out, half_in, full_in,
    local_sems, send_sems, recv_sems,
):
    width, hidden = w_in_ref.shape
    block = width // 16
    dp, tensor = lax.axis_index("dp"), lax.axis_index("tensor")
    xlo, y, core = dp // (2 * Y), (dp // 2) % Y, dp % 2
    z, xhi = tensor // 2, tensor % 2

    def device(xlo, y, core, z, xhi):
        return (xlo * (2 * Y) + y * 2 + core, z * 2 + xhi)

    up = device(xlo, y, core, (z + 1) % Z, xhi)
    down = device(xlo, y, core, (z + Z - 1) % Z, xhi)
    pair = device(1 - xlo, y, core, z, 1 - xhi)
    twin = device(1 - xlo, y, core, z, xhi)
    north = device(xlo, (y + 1) % Y, core, z, xhi)
    south = device(xlo, (y + Y - 1) % Y, core, z, xhi)
    sibling = device(xlo, y, 1 - core, z, xhi)
    everyone = (up, down, pair, twin, north, south, sibling)

    loads = [
        pltpu.make_async_copy(src, dst, local_sems.at[i])
        for i, (src, dst) in enumerate(
            (
                (tokens_ref, tok.at[pl.ds(row_of(OWN, 0, 0), SHARD)]),
                (cotangent_ref, cot.at[pl.ds(row_of(OWN, 0, 0), SHARD)]),
                (w_in_ref, win),
                (w_out_ref, wout),
            )
        )
    ]
    for load in loads:
        load.start()

    barrier = pltpu.get_barrier_semaphore()
    for other in everyone:
        pl.semaphore_signal(barrier, inc=1, device_id=other, device_id_type=MESH)
    pl.semaphore_wait(barrier, len(everyone))

    links = Links(send_sems, recv_sems)
    onward = {BELOW: up, ABOVE: down}

    def slot(buf, side, way, hop, part=slice(0, SHARD)):
        return buf.at[pl.ds(row_of(side, way, hop) + part.start, part.stop - part.start)]

    def first_hop(name, src, buf, side):
        for way in (BELOW, ABOVE):
            links.send((name, side, way, 1), src, slot(buf, side, way, 1), onward[way])

    def relay(name, buf, side, way, hop):
        part = slice(0, SHARD)
        if hop == 3:
            part = slice(0, HALF) if way == BELOW else slice(HALF, SHARD)
        links.send(
            (name, side, way, hop + 1),
            slot(buf, side, way, hop, part),
            slot(buf, side, way, hop + 1, part),
            onward[way],
        )

    links.send(("x", PAIR, 0, 0), tokens_ref, slot(tok, PAIR, 0, 0), pair)
    first_hop("dy", cotangent_ref, cot, OWN)
    first_hop("x", tokens_ref, tok, OWN)
    links.send(("dy", PAIR, 0, 0), cotangent_ref, slot(cot, PAIR, 0, 0), pair)
    links.arrived(("x", PAIR, 0, 0))
    first_hop("x", slot(tok, PAIR, 0, 0), tok, PAIR)

    def forward(chunk):
        rows = pl.ds(chunk * CHUNK, CHUNK)
        for n in range(0, hidden, 256):
            cols = pl.ds(n, 256)
            pre = jnp.dot(tok[rows, :], win[:, cols], preferred_element_type=F32)
            dact = nt(cot[rows, :], wout[cols, :])
            value, slope = gelu_parts(pre)
            change = dact * slope
            dpre[rows, cols] = change.astype(BF16)
            actt[cols, rows] = value.T.astype(BF16)
            dpret[cols, rows] = change.T.astype(BF16)

        def columns(j, carry):
            at = pl.ds(pl.multiple_of(j * 512, 512), 512)
            gx[rows, at] = nt(dpre[rows, :], win[at, :]).astype(BF16)
            return carry

        lax.fori_loop(0, width // 512, columns, 0)

    mid = width // 2
    left, right = pl.ds(0, mid), pl.ds(mid, mid)

    def slot_id(way, hop):
        return 0 if hop == 0 else 7 if hop == 4 else 2 * hop - 1 + way

    def cross(way, hop):
        at = slot_id(way, hop)
        links.send(
            ("gx", PAIR, way, hop),
            gx.at[pl.ds(row_of(PAIR, way, hop), SHARD), right],
            from_pair.at[at],
            pair,
        )

    for hop in (1, 2, 3):
        for way in (BELOW, ABOVE):
            links.arrived(("dy", OWN, way, hop))
            relay("dy", cot, OWN, way, hop)
            links.send(
                ("dy", PAIR, way, hop),
                slot(cot, OWN, way, hop),
                slot(cot, PAIR, way, hop),
                pair,
            )
        for side in (OWN, PAIR):
            for way in (BELOW, ABOVE):
                links.arrived(("x", side, way, hop))
                relay("x", tok, side, way, hop)
        if hop == 1:
            for load in loads:
                load.wait()
            links.arrived(("dy", PAIR, 0, 0))
        else:
            for way in (BELOW, ABOVE):
                links.arrived(("dy", PAIR, way, hop - 1))
            forward(hop - 2)
    for way in (BELOW, ABOVE):
        part = slice(0, HALF) if way == BELOW else slice(HALF, SHARD)
        links.arrived(("dy", OWN, way, 4))
        links.send(
            ("dy", PAIR, way, 4),
            slot(cot, OWN, way, 4, part),
            slot(cot, PAIR, way, 4, part),
            pair,
        )
    for way in (BELOW, ABOVE):
        links.arrived(("dy", PAIR, way, 3))
    forward(2)
    for side in (OWN, PAIR):
        for way in (BELOW, ABOVE):
            links.arrived(("x", side, way, 4))
    for way in (BELOW, ABOVE):
        links.arrived(("dy", PAIR, way, 4))
    forward(3)

    back = {BELOW: down, ABOVE: up}
    pieces = ((OWN, left), (PAIR, left), (OWN, right))

    def add(dst, *others):
        total = dst[...].astype(F32)
        for other in others:
            total = total + other[...].astype(F32)
        dst[...] = total.astype(BF16)

    def hop_back(way, hop):
        if hop == 4:
            part = slice(0, HALF) if way == BELOW else slice(HALF, SHARD)
        else:
            part = slice(0, SHARD)
        for i, (side, cols) in enumerate(pieces):
            mine = gx.at[pl.ds(row_of(side, way, hop) + part.start, part.stop - part.start), cols]
            links.send(
                ("gz", i, way, hop),
                mine,
                from_z.at[i, way, hop - 1, pl.ds(part.start, part.stop - part.start)],
                back[way],
            )

    def take_in(way, hop):
        for i, (side, cols) in enumerate(pieces):
            part = slice(0, SHARD)
            if hop == 3:
                part = slice(0, HALF) if way == BELOW else slice(HALF, SHARD)
            links.arrived(("gz", i, way, hop + 1))
            rows = pl.ds(part.start, part.stop - part.start)
            add(
                gx.at[pl.ds(row_of(side, way, hop) + part.start, part.stop - part.start), cols],
                from_z.at[i, way, hop, rows],
            )

    def take_pair(way, hop):
        links.arrived(("gx", PAIR, way, hop))
        add(
            gx.at[pl.ds(row_of(OWN, way, hop), SHARD), right],
            from_pair.at[slot_id(way, hop)],
        )

    cross(0, 4)
    for hop in (3, 2, 1):
        for way in (BELOW, ABOVE):
            cross(way, hop)
    cross(0, 0)

    IN, OUT = 0, 1

    def product(array, dx, dy, dc):
        there = ((xlo + dx) % 2) * (2 * Y) + ((y + dy) % Y) * 2 + (core + dc) % 2
        cols = pl.ds(pl.multiple_of(there * block, block), block)
        lhs, rhs = (dpret, tok) if array == IN else (actt, cot)
        return jnp.dot(lhs[...], rhs[:, cols], preferred_element_type=F32)

    def to_sibling(array, dx, dy):
        core_out[array, dx, dy] = product(array, dx, dy, 1).astype(BF16)
        links.send(
            ("core", array, dx, dy),
            core_out.at[array, dx, dy],
            core_in.at[array, dx, dy],
            sibling,
        )

    def chip_sum(array, dx, dy):
        mine = product(array, dx, dy, 0)
        links.arrived(("core", array, dx, dy))
        return mine + core_in[array, dx, dy].astype(F32)

    rank = {0: 0, 1: 1, 2: 2, 3: 3}
    mid_h = hidden // 2
    h_lo, h_hi = pl.ds(0, mid_h), pl.ds(mid_h, mid_h)

    def y_far(tag, buf):
        links.send(("half", tag, 0), buf.at[h_lo], half_in.at[tag, 0], north)
        links.send(("half", tag, 1), buf.at[h_hi], half_in.at[tag, 1], south)

    def y_near(tag, side, buf, value):
        links.arrived(("half", tag, side))
        extra = half_in[tag, side].astype(F32)
        if side == 0:
            buf[h_lo] = (value[:mid_h] + extra).astype(BF16)
            buf[h_hi] = value[mid_h:].astype(BF16)
        else:
            buf[h_lo] = value[:mid_h].astype(BF16)
            buf[h_hi] = (value[mid_h:] + extra).astype(BF16)
        links.send(("full", tag, side), buf, full_in.at[tag, side], (north, south)[side])

    def y_sum(tag, value):
        for side in (0, 1):
            links.arrived(("full", tag, side))
            value = value + full_in[tag, side].astype(F32)
        return value

    for dy in (2, 1, 3, 0):
        to_sibling(IN, 1, dy)
    for dx in (1, 0):
        to_sibling(OUT, dx, 2)
    take_pair(0, 4)
    for way in (BELOW, ABOVE):
        hop_back(way, 4)
    for n, dy in enumerate((2, 1, 3, 0)):
        part_in[1, dy] = chip_sum(IN, 1, dy).astype(BF16)
        links.send(("xl", IN, dy), part_in.at[1, dy], xl_in.at[dy], twin)
        if n < 2:
            dx = 1 - n
            part_out[dx, 2] = chip_sum(OUT, dx, 2).astype(BF16)
            y_far(dx, part_out.at[dx, 2])
    for dx in (1, 0):
        for dy in (1, 3):
            to_sibling(OUT, dx, dy)
    for way in (BELOW, ABOVE):
        take_pair(way, 3)
        take_in(way, 3)
        hop_back(way, 3)
    for dx in (1, 0):
        for side, dy in enumerate((1, 3)):
            y_near(dx, side, part_out.at[dx, dy], chip_sum(OUT, dx, dy))
    for dy in (2, 1, 3, 0):
        to_sibling(IN, 0, dy)
    for dx in (1, 0):
        to_sibling(OUT, dx, 0)

    def both_x(dy):
        value = chip_sum(IN, 0, dy)
        links.arrived(("xl", IN, dy))
        return value + xl_in[dy].astype(F32)

    part_in[0, 2] = both_x(2).astype(BF16)
    y_far(2, part_in.at[0, 2])
    for way in (BELOW, ABOVE):
        take_pair(way, 2)
        take_in(way, 2)
        hop_back(way, 2)
    part_out[1, 0] = y_sum(1, chip_sum(OUT, 1, 0)).astype(BF16)
    links.send(("xl", OUT), part_out.at[1, 0], xl_out, twin)
    for side, dy in enumerate((1, 3)):
        y_near(2, side, part_in.at[0, dy], both_x(dy))
    for way in (BELOW, ABOVE):
        take_pair(way, 1)
        take_in(way, 1)
        hop_back(way, 1)

    scale = 1.0 / math.sqrt(16 * 16 * SHARD)
    last = y_sum(0, chip_sum(OUT, 0, 0))
    links.arrived(("xl", OUT))
    gout_ref[...] = ((last + xl_out[...].astype(F32)) * scale).astype(BF16)

    take_pair(0, 0)
    for way in (BELOW, ABOVE):
        take_in(way, 0)
    at = pl.ds(row_of(PAIR, 0, 0), SHARD)
    links.send(("gx end",), gx.at[at, left], from_pair_end, pair)

    last = y_sum(2, both_x(0))
    gin_ref[...] = (last * scale).T.astype(BF16)

    at = pl.ds(row_of(OWN, 0, 0), SHARD)
    gtok_ref[:, right] = gx[at, right]
    links.arrived(("gx end",))
    gtok_ref[:, left] = (gx[at, left].astype(F32) + from_pair_end[...].astype(F32)).astype(BF16)

    links.finish()


def local(tokens, cotangent, w_in, w_out):
    width, hidden = w_in.shape
    block = width // 16
    group = 16 * SHARD
    vmem = pltpu.VMEM
    hbm = pl.BlockSpec(memory_space=pl.ANY)
    return pl.pallas_call(
        kernel,
        out_shape=(
            jax.ShapeDtypeStruct((SHARD, width), BF16),
            jax.ShapeDtypeStruct((block, hidden), BF16),
            jax.ShapeDtypeStruct((hidden, block), BF16),
        ),
        in_specs=[hbm] * 4,
        out_specs=(pl.BlockSpec(memory_space=pltpu.VMEM),) * 3,
        scratch_shapes=[
            vmem((group, width), BF16),
            vmem((group, width), BF16),
            vmem((width, hidden), BF16),
            vmem((hidden, width), BF16),
            vmem((group, hidden), BF16),
            vmem((hidden, group), BF16),
            vmem((hidden, group), BF16),
            vmem((group, width), BF16),
            vmem((3, 2, 4, SHARD, width // 2), BF16),
            vmem((8, SHARD, width // 2), BF16),
            vmem((SHARD, width // 2), BF16),
            vmem((2, 2, Y, hidden, block), BF16),
            vmem((2, 2, Y, hidden, block), BF16),
            vmem((2, Y, hidden, block), BF16),
            vmem((2, Y, hidden, block), BF16),
            vmem((Y, hidden, block), BF16),
            vmem((hidden, block), BF16),
            vmem((3, 2, hidden // 2, block), BF16),
            vmem((3, 2, hidden, block), BF16),
            pltpu.SemaphoreType.DMA((4,)),
            pltpu.SemaphoreType.DMA((MESSAGES,)),
            pltpu.SemaphoreType.DMA((MESSAGES,)),
        ],
        compiler_params=pltpu.CompilerParams(
            collective_id=0, has_side_effects=True, vmem_limit_bytes=60 * 2**20
        ),
        cost_estimate=pl.CostEstimate(
            flops=10 * group * width * hidden,
            bytes_accessed=4 * width * hidden,
            transcendentals=group * hidden,
        ),
    )(tokens, cotangent, w_in, w_out)


def solution(mesh):
    placed = (
        P(("dp", "tensor"), None),
        P(("dp", "tensor"), None),
        P(None, "tensor"),
        P("tensor", None),
    )
    return jax.shard_map(
        local,
        mesh=mesh,
        in_specs=placed,
        out_specs=(P(("dp", "tensor"), None), P("dp", "tensor"), P("tensor", "dp")),
        check_vma=False,
    )
```

time: 583 us -> 128 us (0.22)
  waiting for transfers between devices: 533 us -> 0 us
  Pallas kernels: 0 us -> 121 us
  matrix products: 29.8 us -> 0 us
  between operations: 13.8 us -> 0.64 us
    reduce_scatter x3 -> x0, waiting for transfers between devices: 336 us -> none  [the longest x1 214 us: local(): lax.psum_scatter(lax.dot_general(dpre, w_in, (((1,), (1,)), ((), ())), pr...]
    all_gather x2 -> x0, waiting for transfers between devices: 196 us -> none  [the longest x1 102 us: local(): lax.all_gather(tokens, 'tensor', axis=0, tiled=True)]
    pallas_call x0 -> x1, Pallas kernels: none -> 121 us  [local(): pl.pallas_call(kernel, out_shape=(jax.ShapeDtypeStruct((SHARD, width), BF...]
    dot_general x5 -> x0, matrix products: 29.8 us -> none  [the longest x1 6.63 us: weight_grads(): lax.dot_general(act, group_dy, (((0,), (0,)), ((), ())), preferred_elemen...]
  transfers between devices with their start and end apart: 5 -> 0, of which waited for: 5 -> 0; matrix products, arithmetic and copies ran while one was open for 4% -> 0% of each run, Pallas kernels for 0% -> 0%
where the time goes in v1:
time: 128 us; the launch traced here: 127 us
  Pallas kernels  121 us (95%)
  local copies, waits for them, and re-layouts  5.01 us (4%)
    pallas_call x1, Pallas kernels, local(): pl.pallas_call(kernel, out_shape=(jax.ShapeDtypeStruct((SHARD, width), BF...  121 us
    unnamed x3, local copies, waits for them, and re-layouts  5.01 us

profile of v1, /device:TPU:1, one launch (start us, length us, event | category | flops | bytes accessed | tf_op | source)
XLA Modules:
  0.0 127.0 jit_solution(5697356035915335046)
XLA Ops:
  0.6 121.4 %shard_map.67 = (bf16[32,4096]{1,0:T(8,128)(2,1)}, bf16[256,512]{1,0:T(8,128)(2,1)}, bf16[512,256]{1,0:T(8,128)(2,1)}) custom-call(bf16[32,4096]{1,0:T(8,128)(2,1)} %tokens_ref.1, bf16[32,4096]{1,0:T(8,128)(2,1)} %cotangent_ref.1, bf16[4096,512]{1,0:T(8,128)(2,1)} %w_in_ref.1, bf16[512,4096]{1,0:T(8,128)(2,1)} %w_out_ref.1), custom_call_target="tpu_custom_call" | custom-call | flops 10737418240 | bytes 8388608 | tf_op jit(solution)/shard_map/pallas_call | solution.py:393
  122.0 1.7 %copy.10 = bf16[32,4096]{1,0:T(8,128)(2,1)} copy(bf16[32,4096]{1,0:T(8,128)(2,1)} %get-tuple-element.6) | data formatting | bytes 524288
  123.7 1.7 %copy.11 = bf16[256,512]{1,0:T(8,128)(2,1)} copy(bf16[256,512]{1,0:T(8,128)(2,1)} %get-tuple-element.7) | data formatting | bytes 524288
  125.3 1.7 %copy.12 = bf16[512,256]{1,0:T(8,128)(2,1)} copy(bf16[512,256]{1,0:T(8,128)(2,1)} %get-tuple-element.8) | data formatting | bytes 524288

commit v2 on v1

v2 whole, which is shorter than its diff:
```python
import functools
import math

import jax
import jax.numpy as jnp
from jax import lax
from jax.experimental import pallas as pl
from jax.experimental.pallas import tpu as pltpu
from jax.sharding import PartitionSpec as P

MESH = pl.DeviceIdType.MESH
F32, BF16 = jnp.float32, jnp.bfloat16
CUBIC, ROOT = 0.044715, 0.7978845608028654

SHARD = 32
HALF = SHARD // 2
CHUNK = 4 * SHARD
Z, Y = 8, 4
OWN, PAIR = 0, 1
BELOW, ABOVE = 0, 1


def gelu_parts(pre):
    tangent = jnp.tanh(ROOT * (pre + CUBIC * pre * pre * pre))
    value = 0.5 * pre * (1.0 + tangent)
    slope = 0.5 * (1.0 + tangent) + 0.5 * pre * (1.0 - tangent * tangent) * ROOT * (
        1.0 + 3.0 * CUBIC * pre * pre
    )
    return value, slope


def row_of(side, way, hop):
    if hop == 0:
        return 3 * CHUNK + side * SHARD
    if hop == 4:
        return 3 * CHUNK + (2 + side) * SHARD
    return (hop - 1) * CHUNK + (2 * way + side) * SHARD


class Links:
    def __init__(self, send_sems, recv_sems):
        self.send_sems, self.recv_sems = send_sems, recv_sems
        self.copies = {}

    def send(self, key, src, dst, device):
        at = len(self.copies)
        copy = pltpu.make_async_remote_copy(
            src_ref=src,
            dst_ref=dst,
            send_sem=self.send_sems.at[at],
            recv_sem=self.recv_sems.at[at],
            device_id=device,
            device_id_type=MESH,
        )
        copy.start()
        self.copies[key] = copy

    def arrived(self, key):
        self.copies[key].wait_recv()

    def finish(self):
        for copy in self.copies.values():
            copy.wait_send()


MESSAGES = 120
VMEM_LIMIT = 60 * 2**20


def kernel(
    tokens_ref, cotangent_ref, w_in_ref, w_out_ref,
    gtok_ref, gin_ref, gout_ref,
    tok, cot, win, wout, win_t, wout_t, slopes, dpre, actt, dpret, gx,
    from_z_left, from_z_right, from_pair, from_pair_end,
    core_out_in, core_in_in, core_out_out, core_in_out,
    part_in, part_out, xl_in, xl_out, half_in, full_in, half_out, full_out,
    local_sems, send_sems, recv_sems,
):
    width, hidden = w_in_ref.shape
    block = width // 16
    dp, tensor = lax.axis_index("dp"), lax.axis_index("tensor")
    xlo, y, core = dp // (2 * Y), (dp // 2) % Y, dp % 2
    z, xhi = tensor // 2, tensor % 2

    def device(xlo, y, core, z, xhi):
        return (xlo * (2 * Y) + y * 2 + core, z * 2 + xhi)

    up = device(xlo, y, core, (z + 1) % Z, xhi)
    down = device(xlo, y, core, (z + Z - 1) % Z, xhi)
    pair = device(1 - xlo, y, core, z, 1 - xhi)
    twin = device(1 - xlo, y, core, z, xhi)
    north = device(xlo, (y + 1) % Y, core, z, xhi)
    south = device(xlo, (y + Y - 1) % Y, core, z, xhi)
    sibling = device(xlo, y, 1 - core, z, xhi)
    everyone = (up, down, pair, twin, north, south, sibling)

    loads = [
        pltpu.make_async_copy(src, dst, local_sems.at[i])
        for i, (src, dst) in enumerate(
            (
                (tokens_ref, tok.at[pl.ds(row_of(OWN, 0, 0), SHARD)]),
                (cotangent_ref, cot.at[pl.ds(row_of(OWN, 0, 0), SHARD)]),
                (w_in_ref, win),
                (w_out_ref, wout),
            )
        )
    ]
    for load in loads:
        load.start()

    barrier = pltpu.get_barrier_semaphore()
    for other in everyone:
        pl.semaphore_signal(barrier, inc=1, device_id=other, device_id_type=MESH)
    pl.semaphore_wait(barrier, len(everyone))

    links = Links(send_sems, recv_sems)
    onward = {BELOW: up, ABOVE: down}

    def slot(buf, side, way, hop, part=slice(0, SHARD)):
        return buf.at[pl.ds(row_of(side, way, hop) + part.start, part.stop - part.start)]

    near_cols, far_cols = pl.ds(0, width - 512), pl.ds(width - 512, 512)

    def first_hop(name, src, buf, side):
        for way in (BELOW, ABOVE):
            dst = slot(buf, side, way, 1)
            if name == "x" and side == PAIR:
                src, dst = src.at[:, near_cols] if way == BELOW else src, dst.at[:, near_cols]
            links.send((name, side, way, 1), src, dst, onward[way])

    def travels(way, hop):
        if hop < 4:
            return slice(0, SHARD)
        return slice(0, HALF) if way == BELOW else slice(HALF, SHARD)

    def relay(name, buf, side, way, hop):
        part = travels(way, hop + 1)
        src, dst = slot(buf, side, way, hop, part), slot(buf, side, way, hop + 1, part)
        if name == "x" and side == PAIR:
            src, dst = src.at[:, near_cols], dst.at[:, near_cols]
        links.send((name, side, way, hop + 1), src, dst, onward[way])

    def dy_across(way, hop):
        part = travels(way, hop)
        links.send(
            ("dy", PAIR, way, hop),
            slot(cot, OWN, way, hop, part),
            slot(cot, PAIR, way, hop, part),
            pair,
        )

    def x_across(way, hop):
        part = travels(way, hop)
        links.send(
            ("x far", PAIR, way, hop),
            slot(tok, OWN, way, hop, part).at[:, far_cols],
            slot(tok, PAIR, way, hop, part).at[:, far_cols],
            pair,
        )

    links.send(("x", PAIR, 0, 0), tokens_ref, slot(tok, PAIR, 0, 0), pair)
    first_hop("dy", cotangent_ref, cot, OWN)
    first_hop("x", tokens_ref, tok, OWN)
    links.send(("dy", PAIR, 0, 0), cotangent_ref, slot(cot, PAIR, 0, 0), pair)
    loads[3].wait()

    def turn_out(j, carry):
        at = pl.ds(pl.multiple_of(j * 256, 256), 256)
        wout_t[at, :] = wout[:, at].T
        return carry

    lax.fori_loop(0, width // 256, turn_out, 0)
    links.arrived(("x", PAIR, 0, 0))
    first_hop("x", slot(tok, PAIR, 0, 0), tok, PAIR)

    def turn_in(j, carry):
        at = pl.ds(pl.multiple_of(j * 256, 256), 256)
        win_t[:, at] = win[at, :].T
        return carry

    def forward_x(chunk):
        rows = pl.ds(chunk * CHUNK, CHUNK)
        for n in range(0, hidden, 256):
            cols = pl.ds(n, 256)
            pre = jnp.dot(tok[rows, :], win[:, cols], preferred_element_type=F32)
            value, slope = gelu_parts(pre)
            slopes[:, cols] = slope
            actt[cols, rows] = value.T.astype(BF16)

    def forward_dy(chunk):
        rows = pl.ds(chunk * CHUNK, CHUNK)
        for n in range(0, hidden, 256):
            cols = pl.ds(n, 256)
            dact = jnp.dot(cot[rows, :], wout_t[:, cols], preferred_element_type=F32)
            change = dact * slopes[:, cols]
            dpre[rows, cols] = change.astype(BF16)
            dpret[cols, rows] = change.T.astype(BF16)

        def columns(j, carry):
            at = pl.ds(pl.multiple_of(j * 512, 512), 512)
            gx[rows, at] = jnp.dot(
                dpre[rows, :], win_t[:, at], preferred_element_type=F32
            ).astype(BF16)
            return carry

        lax.fori_loop(0, width // 512, columns, 0)

    mid = 7 * width // 16
    left, right = pl.ds(0, mid), pl.ds(mid, width - mid)

    def slot_id(way, hop):
        return 0 if hop == 0 else 7 if hop == 4 else 2 * hop - 1 + way

    def cross(way, hop):
        at = slot_id(way, hop)
        links.send(
            ("gx", PAIR, way, hop),
            gx.at[pl.ds(row_of(PAIR, way, hop), SHARD), right],
            from_pair.at[at],
            pair,
        )

    for hop in (1, 2, 3):
        for way in (BELOW, ABOVE):
            links.arrived(("dy", OWN, way, hop))
            relay("dy", cot, OWN, way, hop)
            dy_across(way, hop)
        for way in (BELOW, ABOVE):
            links.arrived(("x", OWN, way, hop))
            relay("x", tok, OWN, way, hop)
            x_across(way, hop)
        for way in (BELOW, ABOVE):
            links.arrived(("x", PAIR, way, hop))
            relay("x", tok, PAIR, way, hop)
        if hop == 1:
            for load in loads[:3]:
                load.wait()
            links.arrived(("dy", PAIR, 0, 0))
            lax.fori_loop(0, width // 256, turn_in, 0)
        else:
            for way in (BELOW, ABOVE):
                links.arrived(("x far", PAIR, way, hop - 1))
            forward_x(hop - 2)
            for way in (BELOW, ABOVE):
                links.arrived(("dy", PAIR, way, hop - 1))
            forward_dy(hop - 2)
    for way in (BELOW, ABOVE):
        links.arrived(("dy", OWN, way, 4))
        dy_across(way, 4)
    for way in (BELOW, ABOVE):
        links.arrived(("x far", PAIR, way, 3))
    forward_x(2)
    for way in (BELOW, ABOVE):
        links.arrived(("x", OWN, way, 4))
        x_across(way, 4)
    for way in (BELOW, ABOVE):
        links.arrived(("dy", PAIR, way, 3))
    forward_dy(2)
    for way in (BELOW, ABOVE):
        links.arrived(("x", PAIR, way, 4))
        links.arrived(("x far", PAIR, way, 4))
    forward_x(3)
    for way in (BELOW, ABOVE):
        links.arrived(("dy", PAIR, way, 4))
    forward_dy(3)

    back = {BELOW: down, ABOVE: up}
    pieces = ((PAIR, left), (OWN, left), (OWN, right))

    def add(dst, *others):
        total = dst[...].astype(F32)
        for other in others:
            total = total + other[...].astype(F32)
        dst[...] = total.astype(BF16)

    def landing(i, way, hop, part):
        rows = pl.ds(part.start, part.stop - part.start)
        if i == 2:
            return from_z_right.at[way, hop, rows]
        return from_z_left.at[i, way, hop, rows]

    def hop_back(i, way, hop):
        side, cols = pieces[i]
        part = travels(way, hop)
        links.send(
            ("gz", i, way, hop),
            slot(gx, side, way, hop, part).at[:, cols],
            landing(i, way, hop - 1, part),
            back[way],
        )

    def take_in(i, way, hop):
        side, cols = pieces[i]
        part = travels(way, hop + 1)
        links.arrived(("gz", i, way, hop + 1))
        add(slot(gx, side, way, hop, part).at[:, cols], landing(i, way, hop, part))

    def step_back(hop, *which):
        for i in which:
            for way in (BELOW, ABOVE):
                if i == 2:
                    take_pair(way, hop)
                take_in(i, way, hop)
                hop_back(i, way, hop)

    def take_pair(way, hop):
        links.arrived(("gx", PAIR, way, hop))
        add(
            gx.at[pl.ds(row_of(OWN, way, hop), SHARD), right],
            from_pair.at[slot_id(way, hop)],
        )

    cross(0, 4)
    for i in (0, 1):
        for way in (BELOW, ABOVE):
            hop_back(i, way, 4)
    for hop in (3, 2, 1):
        for way in (BELOW, ABOVE):
            cross(way, hop)
    cross(0, 0)

    IN, OUT = 0, 1
    cut = core_out_in.shape[2]
    core_out, core_in = (core_out_in, core_out_out), (core_in_in, core_in_out)

    def product(array, dx, dy, dc):
        there = ((xlo + dx) % 2) * (2 * Y) + ((y + dy) % Y) * 2 + (core + dc) % 2
        cols = pl.ds(pl.multiple_of(there * block, block), block)
        x, dy_cols = tok[:, cols], cot[:, cols]
        if array == IN:
            return (jnp.dot(dpret[:cut, :], x, preferred_element_type=F32),)
        return (
            jnp.dot(actt[...], dy_cols, preferred_element_type=F32),
            jnp.dot(dpret[cut:, :], x, preferred_element_type=F32),
        )

    def split(array):
        return ((0, cut),) if array == IN else ((0, hidden), (hidden, 2 * hidden - cut))

    def read(ref, array):
        return tuple(ref[a:b].astype(F32) for a, b in split(array))

    def write(ref, array, parts):
        for (a, b), part in zip(split(array), parts):
            ref[a:b] = part.astype(BF16)

    def plus(parts, others):
        return tuple(p + o for p, o in zip(parts, others))

    def to_sibling(array, dx, dy):
        write(core_out[array].at[dx, dy], array, product(array, dx, dy, 1))
        links.send(
            ("core", array, dx, dy),
            core_out[array].at[dx, dy],
            core_in[array].at[dx, dy],
            sibling,
        )

    def chip_sum(array, dx, dy):
        mine = product(array, dx, dy, 0)
        links.arrived(("core", array, dx, dy))
        return plus(mine, read(core_in[array].at[dx, dy], array))

    def half_of(tag):
        return half_in if tag == 2 else half_out.at[tag]

    def full_of(tag):
        return full_in if tag == 2 else full_out.at[tag]

    def y_far(tag, buf):
        rows = buf.shape[0] // 2
        for side, to in enumerate((north, south)):
            links.send(
                ("half", tag, side),
                buf.at[pl.ds(side * rows, rows)],
                half_of(tag).at[side],
                to,
            )

    def y_near(tag, side, buf, array, parts):
        write(buf, array, parts)
        links.arrived(("half", tag, side))
        rows = buf.shape[0] // 2
        add(buf.at[pl.ds(side * rows, rows)], half_of(tag).at[side])
        links.send(("full", tag, side), buf, full_of(tag).at[side], (north, south)[side])

    def y_sum(tag, array, parts):
        for side in (0, 1):
            links.arrived(("full", tag, side))
            parts = plus(parts, read(full_of(tag).at[side], array))
        return parts

    def x_first(dy):
        write(part_in.at[1, dy], IN, chip_sum(IN, 1, dy))
        links.send(("xl", IN, dy), part_in.at[1, dy], xl_in.at[dy], twin)

    def far_out(dx):
        write(part_out.at[dx, 2], OUT, chip_sum(OUT, dx, 2))
        y_far(dx, part_out.at[dx, 2])

    def near_out(dx):
        for side, dy in enumerate((1, 3)):
            y_near(dx, side, part_out.at[dx, dy], OUT, chip_sum(OUT, dx, dy))

    def both_x(dy):
        parts = chip_sum(IN, 0, dy)
        links.arrived(("xl", IN, dy))
        return plus(parts, read(xl_in.at[dy], IN))

    to_sibling(IN, 1, 2)
    to_sibling(IN, 1, 1)
    to_sibling(OUT, 1, 2)
    x_first(2)
    to_sibling(OUT, 0, 2)
    take_pair(0, 4)
    for way in (BELOW, ABOVE):
        hop_back(2, way, 4)
    far_out(1)
    to_sibling(IN, 1, 3)
    x_first(1)
    far_out(0)
    to_sibling(IN, 1, 0)
    x_first(3)
    step_back(3, 0)
    x_first(0)
    step_back(3, 1)
    for dx in (1, 0):
        to_sibling(OUT, dx, 1)
        to_sibling(OUT, dx, 3)
        if dx == 1:
            step_back(3, 2)
    for dy in (2, 1, 3, 0):
        to_sibling(IN, 0, dy)
    near_out(1)
    step_back(2, 0)
    write(part_in.at[0, 2], IN, both_x(2))
    y_far(2, part_in.at[0, 2])
    step_back(2, 1)
    near_out(0)
    for dx in (1, 0):
        to_sibling(OUT, dx, 0)
    step_back(2, 2)
    step_back(1, 0)
    write(part_out.at[1, 0], OUT, y_sum(1, OUT, chip_sum(OUT, 1, 0)))
    links.send(("xl", OUT), part_out.at[1, 0], xl_out, twin)
    step_back(1, 1)
    for side, dy in enumerate((1, 3)):
        y_near(2, side, part_in.at[0, dy], IN, both_x(dy))
    step_back(1, 2)

    at = pl.ds(row_of(PAIR, 0, 0), SHARD)
    for way in (BELOW, ABOVE):
        take_in(0, way, 0)
    links.send(("gx end",), gx.at[at, left], from_pair_end, pair)
    for way in (BELOW, ABOVE):
        take_in(1, way, 0)

    scale = 1.0 / math.sqrt(16 * 16 * SHARD)
    out_parts = y_sum(0, OUT, chip_sum(OUT, 0, 0))
    in_parts = both_x(0)
    take_pair(0, 0)
    for way in (BELOW, ABOVE):
        take_in(2, way, 0)
    at = pl.ds(row_of(OWN, 0, 0), SHARD)
    gtok_ref[:, right] = gx[at, right]
    links.arrived(("gx end",))
    gtok_ref[:, left] = (gx[at, left].astype(F32) + from_pair_end[...].astype(F32)).astype(BF16)

    links.arrived(("xl", OUT))
    grad_out, in_end = plus(out_parts, read(xl_out, OUT))
    gout_ref[...] = (grad_out * scale).astype(BF16)
    gin_ref[:, cut:] = (in_end * scale).T.astype(BF16)
    (in_start,) = y_sum(2, IN, in_parts)
    gin_ref[:, :cut] = (in_start * scale).T.astype(BF16)

    links.finish()


def hand_over(*refs):
    for src, dst in zip(refs[:3], refs[3:]):
        dst[...] = src[...]


def local(tokens, cotangent, w_in, w_out):
    results = layer(tokens, cotangent, w_in, w_out)
    return pl.pallas_call(
        hand_over,
        out_shape=tuple(jax.ShapeDtypeStruct(r.shape, r.dtype) for r in results),
        in_specs=[pl.BlockSpec(memory_space=pltpu.VMEM)] * 3,
        out_specs=(pl.BlockSpec(memory_space=pltpu.VMEM),) * 3,
    )(*results)


def layer(tokens, cotangent, w_in, w_out):
    width, hidden = w_in.shape
    block = width // 16
    group = 16 * SHARD
    mid = 7 * width // 16
    short, long = hidden - 64, hidden + 64
    vmem = pltpu.VMEM
    hbm = pl.BlockSpec(memory_space=pl.ANY)
    return pl.pallas_call(
        kernel,
        out_shape=(
            jax.ShapeDtypeStruct((SHARD, width), BF16),
            jax.ShapeDtypeStruct((block, hidden), BF16),
            jax.ShapeDtypeStruct((hidden, block), BF16),
        ),
        in_specs=[hbm] * 4,
        out_specs=(pl.BlockSpec(memory_space=pltpu.VMEM),) * 3,
        scratch_shapes=[
            vmem((group, width), BF16),
            vmem((group, width), BF16),
            vmem((width, hidden), BF16),
            vmem((hidden, width), BF16),
            vmem((hidden, width), BF16),
            vmem((width, hidden), BF16),
            vmem((CHUNK, hidden), F32),
            vmem((group, hidden), BF16),
            vmem((hidden, group), BF16),
            vmem((hidden, group), BF16),
            vmem((group, width), BF16),
            vmem((2, 2, 4, SHARD, mid), BF16),
            vmem((2, 4, SHARD, width - mid), BF16),
            vmem((8, SHARD, width - mid), BF16),
            vmem((SHARD, mid), BF16),
            vmem((2, Y, short, block), BF16),
            vmem((2, Y, short, block), BF16),
            vmem((2, Y, long, block), BF16),
            vmem((2, Y, long, block), BF16),
            vmem((2, Y, short, block), BF16),
            vmem((2, Y, long, block), BF16),
            vmem((Y, short, block), BF16),
            vmem((long, block), BF16),
            vmem((2, short // 2, block), BF16),
            vmem((2, short, block), BF16),
            vmem((2, 2, long // 2, block), BF16),
            vmem((2, 2, long, block), BF16),
            pltpu.SemaphoreType.DMA((4,)),
            pltpu.SemaphoreType.DMA((MESSAGES,)),
            pltpu.SemaphoreType.DMA((MESSAGES,)),
        ],
        compiler_params=pltpu.CompilerParams(
            collective_id=0, has_side_effects=True, vmem_limit_bytes=VMEM_LIMIT
        ),
        cost_estimate=pl.CostEstimate(
            flops=10 * group * width * hidden,
            bytes_accessed=4 * width * hidden,
            transcendentals=group * hidden,
        ),
    )(tokens, cotangent, w_in, w_out)


def solution(mesh):
    placed = (
        P(("dp", "tensor"), None),
        P(("dp", "tensor"), None),
        P(None, "tensor"),
        P("tensor", None),
    )
    return jax.shard_map(
        local,
        mesh=mesh,
        in_specs=placed,
        out_specs=(P(("dp", "tensor"), None), P("dp", "tensor"), P("tensor", "dp")),
        check_vma=False,
    )
```

time: 128 us -> 117 us (0.914)
  local copies, waits for them, and re-layouts: 5.01 us -> 0 us
  Pallas kernels: 121 us -> 116 us
    pallas_call x1 -> x2, Pallas kernels: 121 us -> 116 us  [the longest x1 114 us: layer(): pl.pallas_call(kernel, out_shape=(jax.ShapeDtypeStruct((SHARD, width), BF...]
    unnamed x3 -> x0, local copies, waits for them, and re-layouts: 5.01 us -> none
where the time goes in v2:
time: 117 us
  Pallas kernels  116 us (99%)
    pallas_call x1, Pallas kernels, layer(): pl.pallas_call(kernel, out_shape=(jax.ShapeDtypeStruct((SHARD, width), BF...  114 us

profile of v2, /device:TPU:1, one launch (start us, length us, event | category | flops | bytes accessed | tf_op | source)
XLA Modules:
  0.0 116.8 jit_solution(11878467424488940674)
XLA Ops:
  0.6 114.2 %shard_map.67 = (bf16[32,4096]{1,0:T(8,128)(2,1)}, bf16[256,512]{1,0:T(8,128)(2,1)}, bf16[512,256]{1,0:T(8,128)(2,1)}) custom-call(bf16[32,4096]{1,0:T(8,128)(2,1)} %tokens_ref.1, bf16[32,4096]{1,0:T(8,128)(2,1)} %cotangent_ref.1, bf16[4096,512]{1,0:T(8,128)(2,1)} %w_in_ref.1, bf16[512,4096]{1,0:T(8,128)(2,1)} %w_out_ref.1), custom_call_target="tpu_custom_call" | custom-call | flops 10737418240 | bytes 8388608 | tf_op jit(solution)/shard_map/pallas_call | solution.py:502
  114.8 2.0 %shard_map.68 = (bf16[32,4096]{1,0:T(8,128)(2,1)}, bf16[256,512]{1,0:T(8,128)(2,1)}, bf16[512,256]{1,0:T(8,128)(2,1)}) custom-call(bf16[32,4096]{1,0:T(8,128)(2,1)} %get-tuple-element.6.refs_0_, bf16[256,512]{1,0:T(8,128)(2,1)} %get-tuple-element.7.refs_1_, bf16[512,256]{1,0:T(8,128)(2,1)} %get-tuple-element.8.refs_2_), custom_call_target="tpu_custom_call" | custom-call | tf_op jit(solution)/shard_map/pallas_call | solution.py:486

commit v3 on v2

--- a/solution.py
+++ b/solution.py
@@ -70,7 +70,7 @@
 def kernel(
     tokens_ref, cotangent_ref, w_in_ref, w_out_ref,
     gtok_ref, gin_ref, gout_ref,
-    tok, cot, win, wout, win_t, wout_t, slopes, dpre, actt, dpret, gx,
+    tok, cot, win, wout, win_t, wout_t, dacts, dpre, actt, dpret, gx,
     from_z_left, from_z_right, from_pair, from_pair_end,
     core_out_in, core_in_in, core_out_out, core_in_out,
     part_in, part_out, xl_in, xl_out, half_in, full_in, half_out, full_out,
@@ -121,12 +121,9 @@
 
     near_cols, far_cols = pl.ds(0, width - 512), pl.ds(width - 512, 512)
 
-    def first_hop(name, src, buf, side):
-        for way in (BELOW, ABOVE):
-            dst = slot(buf, side, way, 1)
-            if name == "x" and side == PAIR:
-                src, dst = src.at[:, near_cols] if way == BELOW else src, dst.at[:, near_cols]
-            links.send((name, side, way, 1), src, dst, onward[way])
+    def first_hop(name, src, buf):
+        for way in (BELOW, ABOVE):
+            links.send((name, OWN, way, 1), src, slot(buf, OWN, way, 1), onward[way])
 
     def travels(way, hop):
         if hop < 4:
@@ -159,8 +156,8 @@
         )
 
     links.send(("x", PAIR, 0, 0), tokens_ref, slot(tok, PAIR, 0, 0), pair)
-    first_hop("dy", cotangent_ref, cot, OWN)
-    first_hop("x", tokens_ref, tok, OWN)
+    first_hop("dy", cotangent_ref, cot)
+    first_hop("x", tokens_ref, tok)
     links.send(("dy", PAIR, 0, 0), cotangent_ref, slot(cot, PAIR, 0, 0), pair)
     loads[3].wait()
 
@@ -171,12 +168,19 @@
 
     lax.fori_loop(0, width // 256, turn_out, 0)
     links.arrived(("x", PAIR, 0, 0))
-    first_hop("x", slot(tok, PAIR, 0, 0), tok, PAIR)
+    for way in (BELOW, ABOVE):
+        relay("x", tok, PAIR, way, 0)
 
     def turn_in(j, carry):
         at = pl.ds(pl.multiple_of(j * 256, 256), 256)
         win_t[:, at] = win[at, :].T
         return carry
+
+    def forward_dy(chunk):
+        rows = pl.ds(chunk * CHUNK, CHUNK)
+        for n in range(0, hidden, 256):
+            cols = pl.ds(n, 256)
+            dacts[:, cols] = jnp.dot(cot[rows, :], wout_t[:, cols], preferred_element_type=F32)
 
     def forward_x(chunk):
         rows = pl.ds(chunk * CHUNK, CHUNK)
@@ -184,17 +188,13 @@
             cols = pl.ds(n, 256)
             pre = jnp.dot(tok[rows, :], win[:, cols], preferred_element_type=F32)
             value, slope = gelu_parts(pre)
-            slopes[:, cols] = slope
-            actt[cols, rows] = value.T.astype(BF16)
-
-    def forward_dy(chunk):
-        rows = pl.ds(chunk * CHUNK, CHUNK)
-        for n in range(0, hidden, 256):
-            cols = pl.ds(n, 256)
-            dact = jnp.dot(cot[rows, :], wout_t[:, cols], preferred_element_type=F32)
-            change = dact * slopes[:, cols]
+            change = dacts[:, cols] * slope
             dpre[rows, cols] = change.astype(BF16)
             dpret[cols, rows] = change.T.astype(BF16)
+            actt[cols, rows] = value.T.astype(BF16)
+
+    def token_part(chunk):
+        rows = pl.ds(chunk * CHUNK, CHUNK)
 
         def columns(j, carry):
             at = pl.ds(pl.multiple_of(j * 512, 512), 512)
@@ -220,49 +220,67 @@
             pair,
         )
 
-    for hop in (1, 2, 3):
+    def dy_step(hop):
         for way in (BELOW, ABOVE):
             links.arrived(("dy", OWN, way, hop))
-            relay("dy", cot, OWN, way, hop)
+            if hop < 4:
+                relay("dy", cot, OWN, way, hop)
             dy_across(way, hop)
+
+    def x_step(hop):
         for way in (BELOW, ABOVE):
             links.arrived(("x", OWN, way, hop))
-            relay("x", tok, OWN, way, hop)
+            if hop < 4:
+                relay("x", tok, OWN, way, hop)
             x_across(way, hop)
-        for way in (BELOW, ABOVE):
-            links.arrived(("x", PAIR, way, hop))
+
+    def all_arrived(name, hop):
+        for way in (BELOW, ABOVE):
+            links.arrived((name, PAIR, way, hop))
+
+    def pair_relay(hop):
+        for way in (BELOW, ABOVE):
             relay("x", tok, PAIR, way, hop)
-        if hop == 1:
-            for load in loads[:3]:
-                load.wait()
-            links.arrived(("dy", PAIR, 0, 0))
-            lax.fori_loop(0, width // 256, turn_in, 0)
-        else:
-            for way in (BELOW, ABOVE):
-                links.arrived(("x far", PAIR, way, hop - 1))
-            forward_x(hop - 2)
-            for way in (BELOW, ABOVE):
-                links.arrived(("dy", PAIR, way, hop - 1))
-            forward_dy(hop - 2)
-    for way in (BELOW, ABOVE):
-        links.arrived(("dy", OWN, way, 4))
-        dy_across(way, 4)
-    for way in (BELOW, ABOVE):
-        links.arrived(("x far", PAIR, way, 3))
+
+    dy_step(1)
+    x_step(1)
+    all_arrived("x", 1)
+    pair_relay(1)
+    for load in loads[:3]:
+        load.wait()
+    links.arrived(("dy", PAIR, 0, 0))
+    lax.fori_loop(0, width // 256, turn_in, 0)
+    dy_step(2)
+    x_step(2)
+    all_arrived("dy", 1)
+    forward_dy(0)
+    all_arrived("x", 2)
+    all_arrived("x far", 1)
+    forward_x(0)
+    token_part(0)
+    dy_step(3)
+    pair_relay(2)
+    all_arrived("dy", 2)
+    forward_dy(1)
+    all_arrived("x far", 2)
+    forward_x(1)
+    x_step(3)
+    dy_step(4)
+    token_part(1)
+    all_arrived("x", 3)
+    pair_relay(3)
+    all_arrived("dy", 3)
+    forward_dy(2)
+    all_arrived("x far", 3)
     forward_x(2)
-    for way in (BELOW, ABOVE):
-        links.arrived(("x", OWN, way, 4))
-        x_across(way, 4)
-    for way in (BELOW, ABOVE):
-        links.arrived(("dy", PAIR, way, 3))
-    forward_dy(2)
-    for way in (BELOW, ABOVE):
-        links.arrived(("x", PAIR, way, 4))
-        links.arrived(("x far", PAIR, way, 4))
+    x_step(4)
+    token_part(2)
+    all_arrived("dy", 4)
+    forward_dy(3)
+    all_arrived("x", 4)
+    all_arrived("x far", 4)
     forward_x(3)
-    for way in (BELOW, ABOVE):
-        links.arrived(("dy", PAIR, way, 4))
-    forward_dy(3)
+    token_part(3)
 
     back = {BELOW: down, ABOVE: up}
     pieces = ((PAIR, left), (OWN, left), (OWN, right))
@@ -407,32 +425,31 @@
         links.arrived(("xl", IN, dy))
         return plus(parts, read(xl_in.at[dy], IN))
 
+    to_sibling(OUT, 1, 2)
     to_sibling(IN, 1, 2)
+    to_sibling(OUT, 0, 2)
     to_sibling(IN, 1, 1)
-    to_sibling(OUT, 1, 2)
+    far_out(1)
     x_first(2)
-    to_sibling(OUT, 0, 2)
+    far_out(0)
+    x_first(1)
+    to_sibling(IN, 1, 3)
+    to_sibling(IN, 1, 0)
+    step_back(3, 0)
+    x_first(3)
+    step_back(3, 1)
+    x_first(0)
     take_pair(0, 4)
     for way in (BELOW, ABOVE):
         hop_back(2, way, 4)
-    far_out(1)
-    to_sibling(IN, 1, 3)
-    x_first(1)
-    far_out(0)
-    to_sibling(IN, 1, 0)
-    x_first(3)
-    step_back(3, 0)
-    x_first(0)
-    step_back(3, 1)
     for dx in (1, 0):
-        to_sibling(OUT, dx, 1)
-        to_sibling(OUT, dx, 3)
-        if dx == 1:
-            step_back(3, 2)
+        for dy in (1, 3):
+            to_sibling(OUT, dx, dy)
     for dy in (2, 1, 3, 0):
         to_sibling(IN, 0, dy)
     near_out(1)
     step_back(2, 0)
+    step_back(3, 2)
     write(part_in.at[0, 2], IN, both_x(2))
     y_far(2, part_in.at[0, 2])
     step_back(2, 1)
@@ -482,13 +499,7 @@
 
 
 def local(tokens, cotangent, w_in, w_out):
-    results = layer(tokens, cotangent, w_in, w_out)
-    return pl.pallas_call(
-        hand_over,
-        out_shape=tuple(jax.ShapeDtypeStruct(r.shape, r.dtype) for r in results),
-        in_specs=[pl.BlockSpec(memory_space=pltpu.VMEM)] * 3,
-        out_specs=(pl.BlockSpec(memory_space=pltpu.VMEM),) * 3,
-    )(*results)
+    return layer(tokens, cotangent, w_in, w_out)
 
 
 def layer(tokens, cotangent, w_in, w_out):
@@ -502,9 +513,9 @@
     return pl.pallas_call(
         kernel,
         out_shape=(
-            jax.ShapeDtypeStruct((SHARD, width), BF16),
-            jax.ShapeDtypeStruct((block, hidden), BF16),
-            jax.ShapeDtypeStruct((hidden, block), BF16),
+            vmem((SHARD, width), BF16),
+            vmem((block, hidden), BF16),
+            vmem((hidden, block), BF16),
         ),
         in_specs=[hbm] * 4,
         out_specs=(pl.BlockSpec(memory_space=pltpu.VMEM),) * 3,

time: 117 us -> 112 us (0.957)
  Pallas kernels: 116 us -> 109 us
  local copies, waits for them, and re-layouts: 0 us -> 2.11 us
    pallas_call x2 -> x1, Pallas kernels: 116 us -> 109 us  [layer(): pl.pallas_call(kernel, out_shape=(vmem((SHARD, width), BF16), vmem((block...]
    unnamed x0 -> x3, local copies, waits for them, and re-layouts: none -> 2.11 us
where the time goes in v3:
time: 112 us
  Pallas kernels  109 us (97%)
  local copies, waits for them, and re-layouts  2.11 us (2%)
    pallas_call x1, Pallas kernels, layer(): pl.pallas_call(kernel, out_shape=(vmem((SHARD, width), BF16), vmem((block...  109 us

profile of v3, /device:TPU:1, one launch (start us, length us, event | category | flops | bytes accessed | tf_op | source)
XLA Modules:
  0.0 111.9 jit_solution(15784138052467683612)
XLA Ops:
  0.6 109.1 %shard_map.67 = (bf16[32,4096]{1,0:T(8,128)(2,1)S(1)}, bf16[256,512]{1,0:T(8,128)(2,1)S(1)}, bf16[512,256]{1,0:T(8,128)(2,1)S(1)}) custom-call(bf16[32,4096]{1,0:T(8,128)(2,1)} %tokens_ref.1, bf16[32,4096]{1,0:T(8,128)(2,1)} %cotangent_ref.1, bf16[4096,512]{1,0:T(8,128)(2,1)} %w_in_ref.1, bf16[512,4096]{1,0:T(8,128)(2,1)} %w_out_ref.1), custom_call_target="tpu_custom_call" | custom-call | flops 10737418240 | bytes 8388608 | tf_op jit(solution)/shard_map/pallas_call | solution.py:513
  109.8 0.7 copy.10
  110.5 0.7 copy.11
  111.2 0.7 copy.12

commit v4 on v3

--- a/solution.py
+++ b/solution.py
@@ -16,6 +16,7 @@
 HALF = SHARD // 2
 CHUNK = 4 * SHARD
 Z, Y = 8, 4
+FAR = 512
 OWN, PAIR = 0, 1
 BELOW, ABOVE = 0, 1
 
@@ -119,7 +120,7 @@
     def slot(buf, side, way, hop, part=slice(0, SHARD)):
         return buf.at[pl.ds(row_of(side, way, hop) + part.start, part.stop - part.start)]
 
-    near_cols, far_cols = pl.ds(0, width - 512), pl.ds(width - 512, 512)
+    near_cols, far_cols = pl.ds(0, width - FAR), pl.ds(width - FAR, FAR)
 
     def first_hop(name, src, buf):
         for way in (BELOW, ABOVE):
@@ -280,7 +281,6 @@
     all_arrived("x", 4)
     all_arrived("x far", 4)
     forward_x(3)
-    token_part(3)
 
     back = {BELOW: down, ABOVE: up}
     pieces = ((PAIR, left), (OWN, left), (OWN, right))
@@ -327,15 +327,6 @@
             gx.at[pl.ds(row_of(OWN, way, hop), SHARD), right],
             from_pair.at[slot_id(way, hop)],
         )
-
-    cross(0, 4)
-    for i in (0, 1):
-        for way in (BELOW, ABOVE):
-            hop_back(i, way, 4)
-    for hop in (3, 2, 1):
-        for way in (BELOW, ABOVE):
-            cross(way, hop)
-    cross(0, 0)
 
     IN, OUT = 0, 1
     cut = core_out_in.shape[2]
@@ -427,27 +418,37 @@
 
     to_sibling(OUT, 1, 2)
     to_sibling(IN, 1, 2)
+    token_part(3)
+    cross(0, 4)
+    for i in (0, 1):
+        for way in (BELOW, ABOVE):
+            hop_back(i, way, 4)
+    far_out(1)
     to_sibling(OUT, 0, 2)
+    x_first(2)
+    for hop in (3, 2, 1):
+        for way in (BELOW, ABOVE):
+            cross(way, hop)
+    cross(0, 0)
     to_sibling(IN, 1, 1)
-    far_out(1)
-    x_first(2)
     far_out(0)
+    to_sibling(IN, 1, 3)
     x_first(1)
-    to_sibling(IN, 1, 3)
     to_sibling(IN, 1, 0)
     step_back(3, 0)
     x_first(3)
-    step_back(3, 1)
-    x_first(0)
     take_pair(0, 4)
     for way in (BELOW, ABOVE):
         hop_back(2, way, 4)
+    step_back(3, 1)
+    x_first(0)
     for dx in (1, 0):
         for dy in (1, 3):
             to_sibling(OUT, dx, dy)
-    for dy in (2, 1, 3, 0):
+    to_sibling(IN, 0, 2)
+    near_out(1)
+    for dy in (1, 3, 0):
         to_sibling(IN, 0, dy)
-    near_out(1)
     step_back(2, 0)
     step_back(3, 2)
     write(part_in.at[0, 2], IN, both_x(2))
@@ -456,19 +457,19 @@
     near_out(0)
     for dx in (1, 0):
         to_sibling(OUT, dx, 0)
-    step_back(2, 2)
     step_back(1, 0)
     write(part_out.at[1, 0], OUT, y_sum(1, OUT, chip_sum(OUT, 1, 0)))
     links.send(("xl", OUT), part_out.at[1, 0], xl_out, twin)
-    step_back(1, 1)
+    step_back(2, 2)
     for side, dy in enumerate((1, 3)):
         y_near(2, side, part_in.at[0, dy], IN, both_x(dy))
-    step_back(1, 2)
+    step_back(1, 1)
 
     at = pl.ds(row_of(PAIR, 0, 0), SHARD)
     for way in (BELOW, ABOVE):
         take_in(0, way, 0)
     links.send(("gx end",), gx.at[at, left], from_pair_end, pair)
+    step_back(1, 2)
     for way in (BELOW, ABOVE):
         take_in(1, way, 0)
 

time: 112 us -> 111 us (level)
  no operation moved by 1% of the time
where the time goes in v4:
time: 111 us
  Pallas kernels  108 us (97%)
  local copies, waits for them, and re-layouts  2.11 us (2%)
    pallas_call x1, Pallas kernels, layer(): pl.pallas_call(kernel, out_shape=(vmem((SHARD, width), BF16), vmem((block...  108 us

profile of v4, /device:TPU:1, one launch (start us, length us, event | category | flops | bytes accessed | tf_op | source)
XLA Modules:
  0.0 111.2 jit_solution(7635219339630208706)
XLA Ops:
  0.6 108.5 %shard_map.67 = (bf16[32,4096]{1,0:T(8,128)(2,1)S(1)}, bf16[256,512]{1,0:T(8,128)(2,1)S(1)}, bf16[512,256]{1,0:T(8,128)(2,1)S(1)}) custom-call(bf16[32,4096]{1,0:T(8,128)(2,1)} %tokens_ref.1, bf16[32,4096]{1,0:T(8,128)(2,1)} %cotangent_ref.1, bf16[4096,512]{1,0:T(8,128)(2,1)} %w_in_ref.1, bf16[512,4096]{1,0:T(8,128)(2,1)} %w_out_ref.1), custom_call_target="tpu_custom_call" | custom-call | flops 10737418240 | bytes 8388608 | tf_op jit(solution)/shard_map/pallas_call | solution.py:514
  109.1 0.7 copy.10
  109.8 0.7 copy.11
  110.5 0.7 copy.12

commit v5 on v4

--- a/solution.py
+++ b/solution.py
@@ -134,7 +134,7 @@
     def relay(name, buf, side, way, hop):
         part = travels(way, hop + 1)
         src, dst = slot(buf, side, way, hop, part), slot(buf, side, way, hop + 1, part)
-        if name == "x" and side == PAIR:
+        if name == "x" and side == PAIR and hop < 3:
             src, dst = src.at[:, near_cols], dst.at[:, near_cols]
         links.send((name, side, way, hop + 1), src, dst, onward[way])
 
@@ -233,7 +233,7 @@
             links.arrived(("x", OWN, way, hop))
             if hop < 4:
                 relay("x", tok, OWN, way, hop)
-            x_across(way, hop)
+                x_across(way, hop)
 
     def all_arrived(name, hop):
         for way in (BELOW, ABOVE):
@@ -246,40 +246,39 @@
     dy_step(1)
     x_step(1)
     all_arrived("x", 1)
-    pair_relay(1)
     for load in loads[:3]:
         load.wait()
     links.arrived(("dy", PAIR, 0, 0))
     lax.fori_loop(0, width // 256, turn_in, 0)
     dy_step(2)
+    pair_relay(1)
     x_step(2)
     all_arrived("dy", 1)
     forward_dy(0)
-    all_arrived("x", 2)
     all_arrived("x far", 1)
     forward_x(0)
     token_part(0)
     dy_step(3)
-    pair_relay(2)
     all_arrived("dy", 2)
     forward_dy(1)
+    all_arrived("x", 2)
+    pair_relay(2)
     all_arrived("x far", 2)
     forward_x(1)
     x_step(3)
     dy_step(4)
     token_part(1)
     all_arrived("x", 3)
+    all_arrived("x far", 3)
     pair_relay(3)
     all_arrived("dy", 3)
     forward_dy(2)
-    all_arrived("x far", 3)
     forward_x(2)
-    x_step(4)
     token_part(2)
     all_arrived("dy", 4)
     forward_dy(3)
+    x_step(4)
     all_arrived("x", 4)
-    all_arrived("x far", 4)
     forward_x(3)
 
     back = {BELOW: down, ABOVE: up}

time: 111 us -> 110 us (level)
    pallas_call x1, Pallas kernels: 108 us -> 107 us  [layer(): pl.pallas_call(kernel, out_shape=(vmem((SHARD, width), BF16), vmem((block...]
where the time goes in v5:
time: 110 us
  Pallas kernels  107 us (97%)
  local copies, waits for them, and re-layouts  2.11 us (2%)
    pallas_call x1, Pallas kernels, layer(): pl.pallas_call(kernel, out_shape=(vmem((SHARD, width), BF16), vmem((block...  107 us

profile of v5, /device:TPU:1, one launch (start us, length us, event | category | flops | bytes accessed | tf_op | source)
XLA Modules:
  0.0 109.5 jit_solution(7529832230458776687)
XLA Ops:
  0.6 106.8 %shard_map.67 = (bf16[32,4096]{1,0:T(8,128)(2,1)S(1)}, bf16[256,512]{1,0:T(8,128)(2,1)S(1)}, bf16[512,256]{1,0:T(8,128)(2,1)S(1)}) custom-call(bf16[32,4096]{1,0:T(8,128)(2,1)} %tokens_ref.1, bf16[32,4096]{1,0:T(8,128)(2,1)} %cotangent_ref.1, bf16[4096,512]{1,0:T(8,128)(2,1)} %w_in_ref.1, bf16[512,4096]{1,0:T(8,128)(2,1)} %w_out_ref.1), custom_call_target="tpu_custom_call" | custom-call | flops 10737418240 | bytes 8388608 | tf_op jit(solution)/shard_map/pallas_call | solution.py:513
  107.4 0.7 copy.10
  108.1 0.7 copy.11
  108.8 0.7 copy.12
